TPU v7x, 256 devices: a whole 4x4x8 slice. The times are simulated.
256 devices in a mesh: fsdp: 32 (over z, y_hi, core), tp: 8 (over y_lo, x).
Axes of the slice: x: 4, y: 4 (y_hi: 2, y_lo: 2; y = y_hi * 2 + y_lo), z: 8, core: 2. Of those that a mesh axis runs over, the one named last changes fastest.
Arguments:
- train_x: bfloat16 [32768, 8192], P('fsdp'), may hold values from -6 to 6
- train_q: bfloat16 [32768, 8192], P('fsdp', 'tp'), may hold values from -17 to 17
- train_k: bfloat16 [32768, 1024], P('fsdp', 'tp'), may hold values from -14 to 14
- train_target: bfloat16 [32768, 8192], P('fsdp', 'tp'), may hold values from -6 to 6
- train_skill: int32 [128], replicated, may hold values from 0 to 3, as said below
- value_weight: bfloat16 [8192, 1024], P('fsdp', 'tp'), may hold values from -0.0625 to 0.0625
- val_x: bfloat16 [4096, 8192], P('fsdp'), may hold values from -6 to 6
- val_q: bfloat16 [4096, 8192], P('fsdp', 'tp'), may hold values from -17 to 17
- val_k: bfloat16 [4096, 1024], P('fsdp', 'tp'), may hold values from -14 to 14
- val_target: bfloat16 [4096, 8192], P('fsdp', 'tp'), may hold values from -6 to 6
- val_skill: int32 [32], replicated, may hold values from 0 to 3, as said below
Outputs:
- skill_grads: bfloat16 [4, 8192, 1024], P(None, 'fsdp', 'tp')
- transfer: float32 [4, 4], replicated
Inputs may be any that keep to these rules, and one draw needn't show every extreme that they name: `train_skill`: each of the 4 skills labels exactly 32 sequences. `val_skill`: each of the 4 skills labels exactly 8 sequences.
All inputs are finite; a program needn't handle non-finite values.
Results may differ from a plain program's by a relative error of at most 0.0052.
The roundings to bfloat16 on the way count: a program that leaves them out, or rounds other values in their place, can miss the bound.
Values may be sent and summed in bfloat16 or wider, within the bound.
No kernel may reach another device: no remote copies, remote signals or barrier semaphores. Data moves between devices by JAX's collectives and lax.ppermute only.
A program may use at most 192 MiB of HBM per device.

v0:
```python
import math
import jax
import jax.numpy as jnp
from jax import lax
from jax.sharding import PartitionSpec as P

HD = 128
SKILLS = 4
SEQ = 256
VSEQ = 128
step_size = 0.01


def attend(query_rows, key_rows, length):
    members = query_rows.shape[0] // length
    kv_heads = key_rows.shape[1] // HD
    group = query_rows.shape[1] // HD // kv_heads
    queries = query_rows.reshape(members, length, kv_heads, group, HD)
    keys = key_rows.reshape(members, length, kv_heads, HD)
    scores = jnp.einsum("bqgrh,bkgh->bgrqk", queries, keys, preferred_element_type=jnp.float32) * (
        1.0 / math.sqrt(HD)
    )
    places = jnp.arange(length)
    allowed = places[:, None] >= places[None, :]
    scores = jnp.where(allowed, scores, jnp.float32(-1e30))
    highest = jnp.max(scores, axis=-1, keepdims=True)
    raised = jnp.exp(scores - highest)
    return (raised / jnp.sum(raised, axis=-1, keepdims=True)).astype(jnp.bfloat16)


def on_device(
    train_x,
    train_q,
    train_k,
    train_target,
    train_skill,
    value_weight,
    val_x,
    val_q,
    val_k,
    val_target,
    val_skill,
):
    head_width = train_k.shape[1]
    kv_heads = head_width // HD
    group = train_q.shape[1] // head_width
    train_rows = train_x.shape[0]
    val_rows = val_x.shape[0]
    train_members = train_rows // SEQ
    val_members = val_rows // VSEQ
    skill_ids = jnp.arange(SKILLS, dtype=jnp.int32)
    shard_rows = lax.all_gather(value_weight, "fsdp", axis=0, tiled=True)
    values = jnp.dot(train_x, shard_rows, preferred_element_type=jnp.float32)
    val_values = jnp.dot(val_x, shard_rows, preferred_element_type=jnp.float32)
    values = values.astype(jnp.bfloat16)
    val_values = val_values.astype(jnp.bfloat16)
    attention = attend(train_q, train_k, SEQ)
    value_blocks = values.reshape(train_members, SEQ, kv_heads, HD)
    mixed = jnp.einsum(
        "bgrqk,bkgh->bqgrh", attention, value_blocks, preferred_element_type=jnp.float32
    )
    target_blocks = train_target.reshape(train_members, SEQ, kv_heads, group, HD).astype(
        jnp.float32
    )
    residual = ((mixed - target_blocks) / SEQ).astype(jnp.bfloat16)
    value_grads = jnp.einsum(
        "bgrqk,bqgrh->bkgh", attention, residual, preferred_element_type=jnp.float32
    )
    grad_rows = value_grads.reshape(train_rows, head_width).astype(jnp.bfloat16)
    train_first = lax.axis_index("fsdp") * train_members
    local_skill = lax.dynamic_slice_in_dim(train_skill, train_first, train_members)
    local_indicator = (local_skill[:, None] == skill_ids[None, :]).astype(jnp.float32)
    running = jnp.zeros(
        (lax.axis_size("fsdp") * (train_x.shape[1] // lax.axis_size("fsdp")), SKILLS, head_width),
        jnp.float32,
    )
    for sequence in range(train_members):
        product = jnp.dot(
            train_x[sequence * SEQ : (sequence + 1) * SEQ].T,
            grad_rows[sequence * SEQ : (sequence + 1) * SEQ],
            preferred_element_type=jnp.float32,
        )
        running = running + local_indicator[sequence][None, :, None] * product[:, None, :]
    shares = lax.psum_scatter(running, "fsdp", scatter_dimension=0, tiled=True)
    skill_grads = jnp.transpose(shares, (1, 0, 2)).astype(jnp.bfloat16)
    val_attention = attend(val_q, val_k, VSEQ)
    val_blocks = val_values.reshape(val_members, VSEQ, kv_heads, HD)
    val_mixed = jnp.einsum(
        "bgrqk,bkgh->bqgrh", val_attention, val_blocks, preferred_element_type=jnp.float32
    )
    val_target_blocks = val_target.reshape(val_members, VSEQ, kv_heads, group, HD).astype(
        jnp.float32
    )
    val_residual = (val_mixed - val_target_blocks) / VSEQ
    val_pull = jnp.einsum(
        "bgrqk,bqgrh->bkgh",
        val_attention.astype(jnp.float32),
        val_residual,
        precision=lax.Precision.HIGHEST,
    )
    val_pull = val_pull.reshape(val_rows, head_width)
    tangent = jnp.einsum(
        "td,sdc->tsc",
        val_x,
        lax.all_gather(skill_grads, "fsdp", axis=1, tiled=True),
        preferred_element_type=jnp.float32,
    )
    along = jnp.einsum("tsc,tc->ts", tangent, val_pull, precision=lax.Precision.HIGHEST)
    val_first = lax.axis_index("fsdp") * val_members
    val_local = lax.dynamic_slice_in_dim(val_skill, val_first, val_members)
    val_indicator = jnp.repeat(
        (val_local[:, None] == skill_ids[None, :]).astype(jnp.float32), VSEQ, axis=0
    )
    partial_transfer = step_size * jnp.dot(along.T, val_indicator, precision=lax.Precision.HIGHEST)
    transfer = lax.psum(partial_transfer, ("fsdp", "tp"))
    return (skill_grads, transfer)


def solution(mesh):
    placed = (
        P("fsdp", None),
        P("fsdp", "tp"),
        P("fsdp", "tp"),
        P("fsdp", "tp"),
        P(),
        P("fsdp", "tp"),
        P("fsdp", None),
        P("fsdp", "tp"),
        P("fsdp", "tp"),
        P("fsdp", "tp"),
        P(),
    )
    return jax.shard_map(
        on_device,
        mesh=mesh,
        in_specs=placed,
        out_specs=(P(None, "fsdp", "tp"), P()),
        check_vma=False,
    )
```

profile of v0, /device:TPU:1, one launch (start us, length us, event | category | flops | bytes accessed | tf_op | source)
XLA Modules:
  0.0 577.4 jit_solution(3521864218452400355)
XLA Ops:
  7.2 0.0 copy-start
  7.2 0.0 all-gather.3.cloned.1.call-start
  7.2 0.7 all-gather.3.cloned.1.call-update
  7.9 0.0 reduce-scatter.2.cloned.1.call-start
  8.0 3.6 copy.56
  11.5 2.0 convert_bitcast_fusion
  13.6 0.0 copy-start.6
  13.6 0.0 copy-start.4
  13.6 2.9 copy.57
  16.5 5.2 copy.28
  21.8 0.0 copy-done.6
  21.8 0.1 dynamic_slice.6
  21.9 0.1 fusion.66
  22.0 0.0 copy-done.4
  22.0 3.1 fusion.1
  25.0 0.0 copy-start.1
  25.0 3.2 copy-done.1
  28.2 1.9 fusion
  30.1 64.9 %all-gather.3.cloned.1.call-done = bf16[8192,128]{1,0:T(8,128)(2,1)} async-done(((bf16[256,128]{1,0:T(8,128)(2,1)}), bf16[8192,128]{1,0:T(8,128)(2,1)}) %all-gather.3.cloned.1.call-update) | async-done | bytes 2097168 | tf_op jit(solution)/shard_map/all_gather | solution.py:52
  95.0 10.8 %convolution_convert_fusion = bf16[1024,128]{1,0:T(8,128)(2,1)S(1)} fusion(bf16[1024,8192]{1,0:T(8,128)(2,1)} %param.11, bf16[8192,128]{1,0:T(8,128)(2,1)} %all-gather.3.cloned.1.call-done), kind=kOutput, calls=%fused_computation.35 | convolution fusion | flops 2147614720 | bytes 19136512 | tf_op jit(solution)/shard_map/dot_general | solution.py:53
  105.9 9.5 %fusion.42 = bf16[4,256,1,128]{1,3,0,2:T(8,128)(2,1)S(1)} fusion(f32[4,8,256]{2,1,0:T(8,128)S(1)} %fusion, f32[4,8,256]{2,1,0:T(8,128)S(1)} %get-tuple-element.6, f32[4,256,256,8]{2,1,3,0:T(8,128)} %copy-done.1, pred[256,256]{0,1:T(8,128)(4,1)S(1)} %iota_compare_fusion, f32[4,256,1,8,128]{1,4,3,0,2:T(8,128)} %copy.28, bf16[4,256,128,1]{2,1,3,0:T(8,128)(2,1)S(1)} %bitcast.216), kind=kOutput, calls=%fused_computation.38 | convolution fusion | flops 1097990144 | bytes 13238272 | tf_op jit(solution)/shard_map/bgrqk,bqgrh->bkgh/dot_general | solution.py:66
  115.4 4.9 convolution_bitcast_fusion
  120.3 4.9 convolution_bitcast_fusion.1
  125.2 4.9 convolution_bitcast_fusion.2
  130.1 4.8 convolution_bitcast_fusion.3
  134.9 5.6 copy.33
  140.5 5.6 copy.32
  146.1 5.6 copy.31
  151.6 5.6 copy.30
  157.2 12.5 %multiply_add_fusion = f32[8192,4,128]{2,0,1:T(8,128)} fusion(f32[8192,128]{1,0:T(8,128)} %copy.33, f32[4]{0:T(128)S(1)} %get-tuple-element.3, f32[8192,128]{1,0:T(8,128)} %copy.32, f32[4]{0:T(128)S(1)} %get-tuple-element.4, f32[8192,128]{1,0:T(8,128)} %copy.31, f32[4]{0:T(128)S(1)} %get-tuple-element.5, f32[8192,128]{1,0:T(8,128)} %copy.30, ...), kind=kLoop, calls=%fused_computation | loop fusion | flops 29360128 | bytes 33554496 | tf_op jit(solution)/shard_map/add | solution.py:83
  169.8 0.0 copy-start.2
  169.8 0.0 copy-start.7
  169.8 0.0 copy-start.3
  169.8 0.0 copy-start.5
  169.8 0.0 reduce-scatter.2.cloned.1.call-update
  169.8 0.0 all-gather.5.cloned.1.call-start
  169.9 212.2 %reduce-scatter.2.cloned.1.call-done = f32[256,4,128]{2,0,1:T(8,128)} async-done(((f32[8192,4,128]{2,0,1:T(8,128)}), f32[256,4,128]{2,0,1:T(8,128)}) %reduce-scatter.2.cloned.1.call-update) | async-done | bytes 524304 | tf_op jit(solution)/shard_map/reduce_scatter | solution.py:84
  382.1 1.8 convert_bitcast_fusion.1
  383.9 0.0 all-gather.5.cloned.1.call-update
  383.9 0.0 copy-done.2
  383.9 0.1 copy.36
  384.1 0.0 copy-done.7
  384.1 0.6 dynamic_slice.7
  384.7 0.6 compare_convert_fusion
  385.3 0.0 copy-done.3
  385.3 0.0 copy-done.5
  385.3 0.2 fusion.72
  385.6 0.1 fusion.59
  385.7 0.0 copy-done
  385.7 3.5 fusion.33
  389.2 1.5 convolution_bitcast_fusion.5
  390.7 99.5 %all-gather.5.cloned.1.call-done = bf16[4,8192,128]{2,1,0:T(8,128)(2,1)} async-done(((bf16[4,256,128]{2,1,0:T(8,128)(2,1)}), bf16[4,8192,128]{2,1,0:T(8,128)(2,1)}) %all-gather.5.cloned.1.call-update) | async-done | bytes 8388624 | tf_op jit(solution)/shard_map/all_gather | solution.py:105
  490.2 5.8 fusion.55
  495.9 0.2 convolution_multiply_fusion.1
  496.1 74.7 %psum.7 = f32[4,4]{1,0:T(4,128)} all-reduce(f32[4,4]{1,0:T(4,128)S(1)} %convolution_multiply_fusion.1), channel_id=1, replica_groups=mesh['fsdp'=32,'tp'=8] {'fsdp','tp'}, use_global_device_ids=true, to_apply=%region_5.6 | all-reduce | flops 16 | bytes 128 | tf_op jit(solution)/shard_map/psum | solution.py:115
  (3 shorter events, 0.0 us)
Async XLA Ops:
  7.2 378.5 %copy-start = (bf16[128,8192]{1,0:T(8,128)(2,1)S(1)}, bf16[128,8192]{1,0:T(8,128)(2,1)}, u32[]{:S(2)}) copy-start(bf16[128,8192]{1,0:T(8,128)(2,1)} %param.17) | copy-start | bytes 6291460
  7.2 87.8 %all-gather.3.cloned.1.call-start = ((), (), s32[]{:S(2)}) async-start(), calls=%async_computation.1 | async-start | bytes 2162688 | tf_op jit(solution)/shard_map/all_gather | solution.py:52
  7.9 374.2 %reduce-scatter.2.cloned.1.call-start = ((), (), s32[]{:S(2)}) async-start(), calls=%async_computation.2 | async-start | bytes 17301504 | tf_op jit(solution)/shard_map/reduce_scatter | solution.py:84
  13.6 8.2 %copy-start.6 = (s32[128]{0:T(128)S(1)}, s32[128]{0:T(128)}, u32[]{:S(2)}) copy-start(s32[128]{0:T(128)} %param.15) | copy-start | bytes 1540
  13.6 8.4 %copy-start.4 = (bf16[1024,128]{1,0:T(8,128)(2,1)S(1)}, bf16[1024,128]{1,0:T(8,128)(2,1)}, u32[]{:S(2)}) copy-start(bf16[1024,128]{1,0:T(8,128)(2,1)} %param.13) | copy-start | bytes 786436
  25.0 3.2 copy-start.1
  169.8 214.1 %copy-start.2 = (bf16[128,1024]{1,0:T(8,128)(2,1)S(1)}, bf16[128,1024]{1,0:T(8,128)(2,1)}, u32[]{:S(2)}) copy-start(bf16[128,1024]{1,0:T(8,128)(2,1)} %param.20) | copy-start | bytes 786436
  169.8 214.3 %copy-start.7 = (s32[32]{0:T(128)S(1)}, s32[32]{0:T(128)}, u32[]{:S(2)}) copy-start(s32[32]{0:T(128)} %param.21) | copy-start | bytes 388
  169.8 215.5 %copy-start.3 = (bf16[128,1024]{1,0:T(8,128)(2,1)S(1)}, bf16[128,1024]{1,0:T(8,128)(2,1)}, u32[]{:S(2)}) copy-start(bf16[128,1024]{1,0:T(8,128)(2,1)} %param.18) | copy-start | bytes 786436
  169.8 215.6 %copy-start.5 = (bf16[128,128]{1,0:T(8,128)(2,1)S(1)}, bf16[128,128]{1,0:T(8,128)(2,1)}, u32[]{:S(2)}) copy-start(bf16[128,128]{1,0:T(8,128)(2,1)} %param.19) | copy-start | bytes 98308
  169.8 320.4 %all-gather.5.cloned.1.call-start = ((), (), s32[]{:S(2)}) async-start(), calls=%async_computation.3 | async-start | bytes 8650752 | tf_op jit(solution)/shard_map/all_gather | solution.py:105
Sparse Core Ops, SparseCore 0:
  10.8 84.1 all-gather.2
  169.9 212.1 reduce-scatter.1
  385.9 104.2 all-gather.4
where the time goes:
time: 578 us; the launch traced here: 577 us
  waiting for transfers between devices  377 us (65%)
  blocking collectives  74.7 us (13%)
  matrix products  54.1 us (9%)
  local copies, waits for them, and re-layouts  38.1 us (7%)
  other arithmetic  19.1 us (3%)
  between operations  13.9 us (2%)
    reduce_scatter x1, waiting for transfers between devices, on_device(): shares = lax.psum_scatter(running, 'fsdp', scatter_dimension=0, tiled=True)  212 us
    all_gather x1, waiting for transfers between devices, on_device(): lax.all_gather(skill_grads, 'fsdp', axis=1, tiled=True)  99.5 us
    psum x1, blocking collectives, on_device(): transfer = lax.psum(partial_transfer, ('fsdp', 'tp'))  74.7 us
    all_gather x1, waiting for transfers between devices, on_device(): shard_rows = lax.all_gather(value_weight, 'fsdp', axis=0, tiled=True)  64.9 us
    dot_general x4, local copies, waits for them, and re-layouts, on_device(): jnp.dot(train_x[sequence * SEQ:(sequence + 1) * SEQ].T, grad_rows[sequenc...  22.3 us
    dot_general x4, matrix products, on_device(): jnp.dot(train_x[sequence * SEQ:(sequence + 1) * SEQ].T, grad_rows[sequenc...  19.5 us
    add x1, other arithmetic, on_device(): running + local_indicator[sequence][None, :, None] * product[:, None, :]  12.5 us
  transfers between devices with their start and end apart: 3, of which 3 were waited for; matrix products, arithmetic and copies ran while one was open for 4% of the time, Pallas kernels for 0%

commit v1 on v0

--- a/solution.py
+++ b/solution.py
@@ -9,6 +9,13 @@
 SEQ = 256
 VSEQ = 128
 step_size = 0.01
+
+
+def exchange_gather(value, name, dim):
+    devices = lax.axis_size(name)
+    blocks = jnp.stack([value for _ in range(devices)])
+    blocks = lax.all_to_all(blocks, name, split_axis=0, concat_axis=0)
+    return jnp.concatenate(blocks, axis=dim)
 
 
 def attend(query_rows, key_rows, length):
@@ -102,7 +109,7 @@
     tangent = jnp.einsum(
         "td,sdc->tsc",
         val_x,
-        lax.all_gather(skill_grads, "fsdp", axis=1, tiled=True),
+        exchange_gather(skill_grads, "fsdp", 1),
         preferred_element_type=jnp.float32,
     )
     along = jnp.einsum("tsc,tc->ts", tangent, val_pull, precision=lax.Precision.HIGHEST)

time: 578 us -> 682 us (1.18)
  waiting for transfers between devices: 377 us -> 457 us
  local copies, waits for them, and re-layouts: 38.1 us -> 51.1 us
  starting transfers between devices: 0.12 us -> 11 us
    all_to_all x0 -> x1, waiting for transfers between devices: none -> 179 us  [exchange_gather(): blocks = lax.all_to_all(blocks, name, split_axis=0, concat_axis=0)]
    all_gather x1 -> x0, waiting for transfers between devices: 99.5 us -> none  [on_device(): lax.all_gather(skill_grads, 'fsdp', axis=1, tiled=True)]
    all_to_all x0 -> x1, starting transfers between devices: none -> 10.9 us  [exchange_gather(): blocks = lax.all_to_all(blocks, name, split_axis=0, concat_axis=0)]
    all_to_all x0 -> x1, local copies, waits for them, and re-layouts: none -> 7.7 us  [exchange_gather(): blocks = lax.all_to_all(blocks, name, split_axis=0, concat_axis=0)]
where the time goes in v1:
time: 682 us; the launch traced here: 681 us
  waiting for transfers between devices  457 us (67%)
  blocking collectives  74.9 us (11%)
  matrix products  54.9 us (8%)
  local copies, waits for them, and re-layouts  51.1 us (7%)
  other arithmetic  18.4 us (3%)
  between operations  14.2 us (2%)
  starting transfers between devices  11 us (2%)
    reduce_scatter x1, waiting for transfers between devices, on_device(): shares = lax.psum_scatter(running, 'fsdp', scatter_dimension=0, tiled=True)  212 us
    all_to_all x1, waiting for transfers between devices, exchange_gather(): blocks = lax.all_to_all(blocks, name, split_axis=0, concat_axis=0)  179 us
    psum x1, blocking collectives, on_device(): transfer = lax.psum(partial_transfer, ('fsdp', 'tp'))  74.9 us
    all_gather x1, waiting for transfers between devices, on_device(): shard_rows = lax.all_gather(value_weight, 'fsdp', axis=0, tiled=True)  64.9 us
    dot_general x4, local copies, waits for them, and re-layouts, on_device(): jnp.dot(train_x[sequence * SEQ:(sequence + 1) * SEQ].T, grad_rows[sequenc...  22.3 us
    dot_general x4, matrix products, on_device(): jnp.dot(train_x[sequence * SEQ:(sequence + 1) * SEQ].T, grad_rows[sequenc...  19.5 us
  transfers between devices with their start and end apart: 3, of which 3 were waited for; matrix products, arithmetic and copies ran while one was open for 4% of the time, Pallas kernels for 0%

profile of v1, /device:TPU:1, one launch (start us, length us, event | category | flops | bytes accessed | tf_op | source)
XLA Modules:
  0.0 681.4 jit_solution(4866205099298088498)
XLA Ops:
  7.2 0.0 copy-start
  7.2 0.0 all-gather.2.cloned.1.call-start
  7.2 0.7 all-gather.2.cloned.1.call-update
  7.9 0.0 reduce-scatter.2.cloned.1.call-start
  8.0 3.6 copy.75
  11.5 2.0 convert_bitcast_fusion
  13.6 0.0 copy-start.6
  13.6 0.0 copy-start.4
  13.6 2.9 copy.76
  16.5 5.2 copy.41
  21.8 0.0 copy-done.6
  21.8 0.1 dynamic_slice.6
  21.9 0.1 fusion.66
  22.0 0.0 copy-done.4
  22.0 3.1 fusion.1
  25.0 0.0 copy-start.1
  25.0 3.2 copy-done.1
  28.2 1.9 fusion
  30.1 64.9 %all-gather.2.cloned.1.call-done = bf16[8192,128]{1,0:T(8,128)(2,1)} async-done(((bf16[256,128]{1,0:T(8,128)(2,1)}), bf16[8192,128]{1,0:T(8,128)(2,1)}) %all-gather.2.cloned.1.call-update) | async-done | bytes 2097168 | tf_op jit(solution)/shard_map/all_gather | solution.py:59
  95.0 10.8 %convolution_convert_fusion = bf16[1024,128]{1,0:T(8,128)(2,1)S(1)} fusion(bf16[1024,8192]{1,0:T(8,128)(2,1)} %param.11, bf16[8192,128]{1,0:T(8,128)(2,1)} %all-gather.2.cloned.1.call-done), kind=kOutput, calls=%fused_computation.35 | convolution fusion | flops 2147614720 | bytes 19136512 | tf_op jit(solution)/shard_map/dot_general | solution.py:60
  105.9 9.5 %fusion.42 = bf16[4,256,1,128]{1,3,0,2:T(8,128)(2,1)S(1)} fusion(f32[4,8,256]{2,1,0:T(8,128)S(1)} %fusion, f32[4,8,256]{2,1,0:T(8,128)S(1)} %get-tuple-element.6, f32[4,256,256,8]{2,1,3,0:T(8,128)} %copy-done.1, pred[256,256]{0,1:T(8,128)(4,1)S(1)} %iota_compare_fusion, f32[4,256,1,8,128]{1,4,3,0,2:T(8,128)} %copy.41, bf16[4,256,128,1]{2,1,3,0:T(8,128)(2,1)S(1)} %bitcast.220), kind=kOutput, calls=%fused_computation.38 | convolution fusion | flops 1097990144 | bytes 13238272 | tf_op jit(solution)/shard_map/bgrqk,bqgrh->bkgh/dot_general | solution.py:73
  115.4 4.9 convolution_bitcast_fusion
  120.3 4.9 convolution_bitcast_fusion.1
  125.2 4.9 convolution_bitcast_fusion.2
  130.1 4.8 convolution_bitcast_fusion.3
  134.9 5.6 copy.46
  140.5 5.6 copy.45
  146.1 5.6 copy.44
  151.6 5.6 copy.43
  157.2 12.5 %multiply_add_fusion = f32[8192,4,128]{2,0,1:T(8,128)} fusion(f32[8192,128]{1,0:T(8,128)} %copy.46, f32[4]{0:T(128)S(1)} %get-tuple-element.3, f32[8192,128]{1,0:T(8,128)} %copy.45, f32[4]{0:T(128)S(1)} %get-tuple-element.4, f32[8192,128]{1,0:T(8,128)} %copy.44, f32[4]{0:T(128)S(1)} %get-tuple-element.5, f32[8192,128]{1,0:T(8,128)} %copy.43, ...), kind=kLoop, calls=%fused_computation | loop fusion | flops 29360128 | bytes 33554496 | tf_op jit(solution)/shard_map/add | solution.py:90
  169.8 0.0 reduce-scatter.2.cloned.1.call-update
  169.8 212.3 %reduce-scatter.2.cloned.1.call-done = f32[256,4,128]{2,0,1:T(8,128)} async-done(((f32[8192,4,128]{2,0,1:T(8,128)}), f32[256,4,128]{2,0,1:T(8,128)}) %reduce-scatter.2.cloned.1.call-update) | async-done | bytes 524304 | tf_op jit(solution)/shard_map/reduce_scatter | solution.py:91
  382.1 1.1 convert_bitcast_fusion.1
  383.2 0.0 copy-start.2
  383.2 5.3 stack.2
  388.5 0.0 copy-start.3
  388.5 0.0 copy-start.7
  388.5 0.0 copy-start.5
  388.5 0.0 copy-done.2
  388.5 10.9 %all-to-all-start = ((bf16[32,4,256,128]{3,2,1,0:T(8,128)(2,1)}), bf16[32,4,256,128]{3,2,1,0:T(8,128)(2,1)}, u32[]{:S(2)}, u32[]{:S(2)}) async-start(bf16[32,4,256,128]{3,2,1,0:T(8,128)(2,1)} %stack.2), calls=%async_computation.1 | async-start | bytes 16777216 | tf_op jit(solution)/shard_map/all_to_all | solution.py:17
  399.4 0.0 copy-done.3
  399.4 0.1 copy.52
  399.6 0.0 copy-done.7
  399.6 0.6 dynamic_slice.7
  400.2 0.6 compare_convert_fusion
  400.8 0.0 copy-done.5
  400.8 1.2 fusion.72
  402.1 0.1 fusion.59
  402.1 0.0 copy-done
  402.2 3.3 fusion.33
  405.5 1.5 convolution_bitcast_fusion.5
  406.9 179.0 %all-to-all-done = bf16[32,4,256,128]{3,2,1,0:T(8,128)(2,1)} async-done(((bf16[32,4,256,128]{3,2,1,0:T(8,128)(2,1)}), bf16[32,4,256,128]{3,2,1,0:T(8,128)(2,1)}, u32[]{:S(2)}, u32[]{:S(2)}) %all-to-all-start) | async-done | bytes 8388640 | tf_op jit(solution)/shard_map/all_to_all | solution.py:17
  586.0 7.7 %copy.47 = bf16[32,4,256,128]{3,2,0,1:T(8,128)(2,1)} copy(bf16[32,4,256,128]{3,2,1,0:T(8,128)(2,1)} %all-to-all-done) | data formatting | bytes 16777216 | tf_op jit(solution)/shard_map/all_to_all | solution.py:17
  593.7 5.8 fusion.55
  599.5 0.2 convolution_multiply_fusion.1
  599.6 74.9 %psum.7 = f32[4,4]{1,0:T(4,128)} all-reduce(f32[4,4]{1,0:T(4,128)S(1)} %convolution_multiply_fusion.1), channel_id=1, replica_groups=mesh['fsdp'=32,'tp'=8] {'fsdp','tp'}, use_global_device_ids=true, to_apply=%region_5.6 | all-reduce | flops 16 | bytes 128 | tf_op jit(solution)/shard_map/psum | solution.py:122
  (3 shorter events, 0.0 us)
Async XLA Ops:
  7.2 395.0 %copy-start = (bf16[128,8192]{1,0:T(8,128)(2,1)S(1)}, bf16[128,8192]{1,0:T(8,128)(2,1)}, u32[]{:S(2)}) copy-start(bf16[128,8192]{1,0:T(8,128)(2,1)} %param.17) | copy-start | bytes 6291460
  7.2 87.8 %all-gather.2.cloned.1.call-start = ((), (), s32[]{:S(2)}) async-start(), calls=%async_computation.2 | async-start | bytes 2162688 | tf_op jit(solution)/shard_map/all_gather | solution.py:59
  7.9 374.2 %reduce-scatter.2.cloned.1.call-start = ((), (), s32[]{:S(2)}) async-start(), calls=%async_computation.3 | async-start | bytes 17301504 | tf_op jit(solution)/shard_map/reduce_scatter | solution.py:91
  13.6 8.2 %copy-start.6 = (s32[128]{0:T(128)S(1)}, s32[128]{0:T(128)}, u32[]{:S(2)}) copy-start(s32[128]{0:T(128)} %param.15) | copy-start | bytes 1540
  13.6 8.4 %copy-start.4 = (bf16[1024,128]{1,0:T(8,128)(2,1)S(1)}, bf16[1024,128]{1,0:T(8,128)(2,1)}, u32[]{:S(2)}) copy-start(bf16[1024,128]{1,0:T(8,128)(2,1)} %param.13) | copy-start | bytes 786436
  25.0 3.2 copy-start.1
  383.2 5.3 copy-start.2
  388.5 10.9 %copy-start.3 = (bf16[128,1024]{1,0:T(8,128)(2,1)S(1)}, bf16[128,1024]{1,0:T(8,128)(2,1)}, u32[]{:S(2)}) copy-start(bf16[128,1024]{1,0:T(8,128)(2,1)} %param.20) | copy-start | bytes 786436
  388.5 11.1 %copy-start.7 = (s32[32]{0:T(128)S(1)}, s32[32]{0:T(128)}, u32[]{:S(2)}) copy-start(s32[32]{0:T(128)} %param.21) | copy-start | bytes 388
  388.5 12.4 %copy-start.5 = (bf16[128,128]{1,0:T(8,128)(2,1)S(1)}, bf16[128,128]{1,0:T(8,128)(2,1)}, u32[]{:S(2)}) copy-start(bf16[128,128]{1,0:T(8,128)(2,1)} %param.19) | copy-start | bytes 98308
  388.5 197.5 %all-to-all-start = ((bf16[32,4,256,128]{3,2,1,0:T(8,128)(2,1)}), bf16[32,4,256,128]{3,2,1,0:T(8,128)(2,1)}, u32[]{:S(2)}, u32[]{:S(2)}) async-start(bf16[32,4,256,128]{3,2,1,0:T(8,128)(2,1)} %stack.2), calls=%async_computation.1 | async-start | bytes 16777216 | tf_op jit(solution)/shard_map/all_to_all | solution.py:17
Sparse Core Ops, SparseCore 0:
  10.8 84.1 all-gather.1
  169.9 212.1 reduce-scatter.1
